TPU v7x, 32 devices: a whole 2x2x4 slice. The times are simulated.
32 devices in a mesh: tpair: 8 (over z, x), col: 4 (over y, core).
Axes of the slice: x: 2, y: 2, z: 4, core: 2. Of those that a mesh axis runs over, the one named last changes fastest.
Arguments:
- peramb: bfloat16 [8, 2, 2048, 2048], P('tpair', None, None, 'col'), may hold values from -6 to 6
- sink_ops: bfloat16 [8, 2, 2, 512, 512], P('tpair'), may hold values from -0.1875 to 0.1875
- op_table: bfloat16 [2048, 2, 512], P('tpair'), may hold values from -0.1875 to 0.1875
- row_slot: int32 [2048], replicated, may hold values from 0 to 2047, each once
- pair_source: int32 [8], P('tpair'), may hold values from 0 to 1
- op_index: int32 [16, 2], P('tpair'), may hold values from 0 to 1
- listed_rows: int32 [16, 128], P('tpair'), may hold values from 0 to 511
Outputs:
- contracted: bfloat16 [16, 4, 128, 2, 2048], P('tpair', None, 'col')
Inputs may be any that keep to these rules, and one draw needn't show every extreme that they name: `row_slot`: every position of 0 to 2047 appears once.
All inputs are finite; a program needn't handle non-finite values.
Results may differ from a plain program's by a relative error of at most 0.0049.
Values may be sent and summed in bfloat16 or wider, within the bound.
No kernel may reach another device: no remote copies, remote signals or barrier semaphores. Data moves between devices by JAX's collectives and lax.ppermute only.
A program may use at most 64 MiB of HBM per device.

v0:
```python
import jax
import jax.numpy as jnp
from jax import lax
from jax.sharding import PartitionSpec as P

NS = 4


def per_device(peramb, sink_ops, op_table, row_slot, pair_source, op_index, listed_rows):
    n_cols = lax.axis_size("col")
    eigen = op_table.shape[2]
    nops = sink_ops.shape[1]
    gathered = lax.all_gather(op_table, "tpair", axis=0, tiled=True)
    listed = listed_rows.shape[1]
    products = op_index.shape[0]
    left = sink_ops[0][op_index[:, 0:1], :, listed_rows]
    source_rows = (pair_source[0] * nops + op_index[:, 1:2]) * eigen
    right_pos = row_slot[source_rows + jnp.arange(eigen, dtype=jnp.int32)[None, :]]
    right = gathered[right_pos]
    left_re = left[:, :, 0]
    left_im = left[:, :, 1]
    left_block = jnp.stack([jnp.stack([left_re, -left_im], 2), jnp.stack([left_im, left_re], 2)], 1)
    local_cols = peramb.shape[3]
    spin_cols = peramb[0].reshape(2, NS, eigen, local_cols)
    mixed = jnp.einsum(
        "pjirv,rsvc->pjsic", left_block, spin_cols, preferred_element_type=jnp.float32
    )
    mixed = mixed.astype(jnp.bfloat16)
    own_rows = listed // n_cols
    order_full = NS * eigen
    right_re = right[:, :, 0]
    right_im = right[:, :, 1]
    right_block = jnp.stack(
        [jnp.stack([right_re, right_im], 2), jnp.stack([-right_im, right_re], 2)], 1
    )
    regrouped = lax.all_to_all(mixed, "col", split_axis=3, concat_axis=4, tiled=True)
    spins = regrouped.shape[2]
    split = regrouped.reshape(products, 2, spins, own_rows, NS, eigen)
    result = jnp.einsum(
        "pjsitv,pjvow->psiotw", split, right_block, preferred_element_type=jnp.float32
    )
    return result.reshape(products, spins, own_rows, 2, order_full).astype(jnp.bfloat16)


def solution(mesh):
    in_specs = (
        P("tpair", None, None, "col"),
        P("tpair", None, None, None, None),
        P("tpair", None, None),
        P(),
        P("tpair"),
        P("tpair", None),
        P("tpair", None),
    )
    out_specs = P("tpair", None, "col", None, None)
    return jax.shard_map(
        per_device, mesh=mesh, in_specs=in_specs, out_specs=out_specs, check_vma=False
    )
```

profile of v0, /device:TPU:0, one launch (start us, length us, event | category | flops | bytes accessed | tf_op | source)
XLA Modules:
  0.0 114.7 jit_solution(943569647819875617)
XLA Ops:
  6.5 0.0 copy-start
  6.5 0.0 all-gather.2.cloned.1.call-start
  6.5 0.7 all-gather.2.cloned.1.call-update
  7.9 0.0 copy-start.2
  7.9 0.0 copy-start.3
  7.9 3.8 %copy.94 = bf16[1,2,2,512,512]{4,2,3,1,0:T(2,128)(2,1)S(1)} copy(bf16[1,2,2,512,512]{4,3,2,1,0:T(8,128)(2,1)} %param.8) | data formatting | bytes 4194304 | tf_op args[1]
  11.7 0.0 copy-done.2
  11.7 0.2 multiply_reduce_fusion
  11.9 0.0 copy-done.3
  11.9 0.1 fusion.22
  12.0 2.0 %gather_fusion.2 = bf16[256,2,512]{2,1,0:T(2,128)(2,1)S(1)} fusion(bf16[2,2,512,512]{3,1,2,0:T(2,128)(2,1)S(1)} %bitcast.92, s32[256]{0:T(256)S(1)} %fusion.22), kind=kCustom, calls=%fused_computation.2 | custom fusion | bytes 1050624 | tf_op jit(solution)/shard_map/gather | solution.py:16
  14.0 0.0 copy-start.4
  14.0 0.1 copy.57
  14.1 0.1 maximum_bitcast_fusion.7
  14.2 2.0 %copy-done.4 = bf16[1,2,2048,512]{3,2,1,0:T(8,128)(2,1)S(1)} copy-done((bf16[1,2,2048,512]{3,2,1,0:T(8,128)(2,1)S(1)}, bf16[1,2,2048,512]{3,2,1,0:T(8,128)(2,1)}, u32[]{:S(2)}) %copy-start.4) | copy-done | bytes 4194328
  16.2 2.4 %fusion.8 = bf16[2,2,4,128,512]{4,3,2,1,0:T(8,128)(2,1)S(1)} fusion(bf16[2,4,512,512,1,1]{3,2,1,0,5,4:T(8,128)(2,1)S(1)} %bitcast.97, bf16[2,1,128,2,512]{4,2,3,1,0:T(8,128)(2,1)S(1)} %get-tuple-element.10, bf16[2,1,128,2,512]{4,2,3,1,0:T(8,128)(2,1)S(1)} %get-tuple-element.9), kind=kOutput, calls=%fused_computation.14 | convolution fusion | flops 2150629376 | bytes 7340032 | tf_op jit(solution)/shard_map/pjirv,rsvc->pjsic/dot_general | solution.py:25
  18.5 2.9 %copy.62 = bf16[2,2,4,128,512]{4,2,1,0,3:T(4,128)(2,1)} copy(bf16[2,2,4,128,512]{4,3,2,1,0:T(8,128)(2,1)S(1)} %fusion.8) | data formatting | bytes 4194304 | tf_op jit(solution)/shard_map/convert_element_type | solution.py:28
  21.5 4.6 %all-to-all-start = ((bf16[2,2,4,128,512]{4,2,1,0,3:T(4,128)(2,1)}), bf16[2,2,4,128,512]{4,2,1,0,3:T(4,128)(2,1)}, u32[]{:S(2)}, u32[]{:S(2)}) async-start(bf16[2,2,4,128,512]{4,2,1,0,3:T(4,128)(2,1)} %copy.62), calls=%async_computation | async-start | bytes 4194304 | tf_op jit(solution)/shard_map/all_to_all | solution.py:36
  26.1 0.1 fusion.14
  26.2 6.2 %gather_fusion = s32[1024]{0:T(1024)S(1)} fusion(s32[2048]{0:T(1024)S(1)} %copy-done, s32[1024]{0:T(1024)S(1)} %broadcast_clamp_fusion), kind=kCustom, calls=%fused_computation | custom fusion | bytes 12288 | tf_op jit(solution)/shard_map/gather | solution.py:18
  32.4 53.2 %all-gather.2.cloned.1.call-done = bf16[2048,2,512]{2,1,0:T(2,128)(2,1)} async-done(((bf16[256,2,512]{2,1,0:T(2,128)(2,1)}), bf16[2048,2,512]{2,1,0:T(2,128)(2,1)}) %all-gather.2.cloned.1.call-update) | async-done | bytes 4194320 | tf_op jit(solution)/shard_map/all_gather | solution.py:13
  85.6 8.1 %gather_fusion.1 = bf16[1024,2,512]{2,1,0:T(2,128)(2,1)S(1)} fusion(bf16[2048,2,512]{2,1,0:T(2,128)(2,1)} %all-gather.2.cloned.1.call-done, s32[1024]{0:T(1024)S(1)} %broadcast_clamp_fusion.1), kind=kCustom, calls=%fused_computation.1 | custom fusion | bytes 4198400 | tf_op jit(solution)/shard_map/gather | solution.py:19
  93.7 0.3 copy.52
  94.0 1.7 %copy.55 = bf16[2,1,512,2,512]{4,2,1,3,0:T(8,128)(2,1)} copy(bf16[2,1,512,2,512]{4,3,2,0,1:T(2,128)(2,1)S(1)} %bitcast.89) | data formatting | bytes 4194304 | tf_op jit(solution)/shard_map/stack | solution.py:33
  95.7 0.1 fusion.9
  95.8 0.1 slice_bitcast_fusion
  95.8 1.5 %maximum_bitcast_fusion.4 = bf16[2,1,512,2,512]{4,2,1,3,0:T(8,128)(2,1)} fusion(bf16[2,512,1,512]{3,1,2,0:T(8,128)(2,1)S(1)} %slice_bitcast_fusion, bf16[2,512,1,512]{3,1,2,0:T(8,128)(2,1)S(1)} %fusion.9), kind=kLoop, calls=%fused_computation.9 | loop fusion | flops 1048576 | bytes 4194304 | tf_op jit(solution)/shard_map/stack | solution.py:33
  97.4 0.0 all-to-all-done
  97.4 0.8 copy-done.1
  98.2 5.8 %fusion.5 = bf16[2,4,32,2,4,512]{5,2,4,1,3,0:T(8,128)(2,1)S(1)} fusion(bf16[2,2,4,4,32,512]{5,2,1,0,4,3:T(4,128)(2,1)} %bitcast.20, bf16[2,1,512,2,512]{4,2,1,3,0:T(8,128)(2,1)} %maximum_bitcast_fusion.4, bf16[2,1,512,2,512]{4,2,1,3,0:T(8,128)(2,1)S(1)} %copy-done.1), kind=kOutput, calls=%fused_computation.13 | convolution fusion | flops 2156920832 | bytes 8388608 | tf_op jit(solution)/shard_map/pjsitv,pjvow->psiotw/dot_general | solution.py:39
  104.0 1.6 %copy.79 = bf16[2,4,32,2,4,512]{5,4,3,2,1,0:T(4,128)(2,1)S(1)} copy(bf16[2,4,32,2,4,512]{5,2,4,1,3,0:T(8,128)(2,1)S(1)} %fusion.5) | data formatting | bytes 4194304 | tf_op jit(solution)/shard_map/convert_element_type | solution.py:42
  105.6 2.2 %reshape.106 = bf16[2,4,32,2,2048]{4,3,2,1,0:T(2,128)(2,1)} reshape(bf16[2,4,32,2,4,512]{5,4,3,2,1,0:T(4,128)(2,1)S(1)} %copy.79) | data formatting | bytes 4194304 | tf_op jit(solution)/shard_map/convert_element_type | solution.py:42
  (10 shorter events, 0.1 us)
Async XLA Ops:
  6.5 19.7 %copy-start = (s32[2048]{0:T(1024)S(1)}, s32[2048]{0:T(1024)}, u32[]{:S(2)}) copy-start(s32[2048]{0:T(1024)} %param.10) | copy-start | bytes 24580
  6.5 79.1 %all-gather.2.cloned.1.call-start = ((), (), s32[]{:S(2)}) async-start(), calls=%async_computation.1 | async-start | bytes 4718592 | tf_op jit(solution)/shard_map/all_gather | solution.py:13
  7.9 3.8 %copy-start.2 = (s32[2,2]{1,0:T(2,128)S(1)}, s32[2,2]{1,0:T(2,128)}, u32[]{:S(2)}) copy-start(s32[2,2]{1,0:T(2,128)} %param.12) | copy-start | bytes 52
  7.9 4.0 %copy-start.3 = (s32[2,128]{1,0:T(2,128)S(1)}, s32[2,128]{1,0:T(2,128)}, u32[]{:S(2)}) copy-start(s32[2,128]{1,0:T(2,128)} %param.13) | copy-start | bytes 3076
  14.0 2.2 %copy-start.4 = (bf16[1,2,2048,512]{3,2,1,0:T(8,128)(2,1)S(1)}, bf16[1,2,2048,512]{3,2,1,0:T(8,128)(2,1)}, u32[]{:S(2)}) copy-start(bf16[1,2,2048,512]{3,2,1,0:T(8,128)(2,1)} %param.7) | copy-start | bytes 12582916
  21.5 75.9 %all-to-all-start = ((bf16[2,2,4,128,512]{4,2,1,0,3:T(4,128)(2,1)}), bf16[2,2,4,128,512]{4,2,1,0,3:T(4,128)(2,1)}, u32[]{:S(2)}, u32[]{:S(2)}) async-start(bf16[2,2,4,128,512]{4,2,1,0,3:T(4,128)(2,1)} %copy.62), calls=%async_computation | async-start | bytes 4194304 | tf_op jit(solution)/shard_map/all_to_all | solution.py:36
  95.8 2.3 %copy-start.1 = (bf16[2,1,512,2,512]{4,2,1,3,0:T(8,128)(2,1)S(1)}, bf16[2,1,512,2,512]{4,2,1,3,0:T(8,128)(2,1)}, u32[]{:S(2)}) copy-start(bf16[2,1,512,2,512]{4,2,1,3,0:T(8,128)(2,1)} %copy.55) | copy-start | bytes 6291460
Sparse Core Ops, SparseCore 0:
  9.5 76.0 all-gather.1
where the time goes:
time: 115 us
  waiting for transfers between devices  53.9 us (47%)
  local copies, waits for them, and re-layouts  31.7 us (28%)
  between operations  14.2 us (12%)
  matrix products  8.13 us (7%)
  starting transfers between devices  4.64 us (4%)
  other arithmetic  2.04 us (2%)
    all_gather x1, waiting for transfers between devices, per_device(): gathered = lax.all_gather(op_table, 'tpair', axis=0, tiled=True)  53.2 us
    gather x2, local copies, waits for them, and re-layouts, per_device(): right = gathered[right_pos]  8.39 us
    unnamed x15, local copies, waits for them, and re-layouts  6.66 us
    gather x2, local copies, waits for them, and re-layouts, per_device(): row_slot[source_rows + jnp.arange(eigen, dtype=jnp.int32)[None, :]]  6.16 us
    dot_general x1, matrix products, per_device(): jnp.einsum('pjsitv,pjvow->psiotw', split, right_block, preferred_element_...  5.77 us
    all_to_all x1, starting transfers between devices, per_device(): lax.all_to_all(mixed, 'col', split_axis=3, concat_axis=4, tiled=True)  4.63 us
    convert_element_type x2, local copies, waits for them, and re-layouts, per_device(): result.reshape(products, spins, own_rows, 2, order_full)  3.84 us
    convert_element_type x1, local copies, waits for them, and re-layouts, per_device(): mixed = mixed.astype(jnp.bfloat16)  2.94 us
  transfers between devices with their start and end apart: 2, of which 1 were waited for; matrix products, arithmetic and copies ran while one was open for 26% of the time, Pallas kernels for 0%

commit v1 on v0

v1 whole, which is shorter than its diff:
```python
import functools

import jax
import jax.numpy as jnp
from jax import lax
from jax.experimental import pallas as pl
from jax.experimental.pallas import tpu as pltpu
from jax.sharding import PartitionSpec as P

NS = 4
VMEM_LIMIT = 56 * 1024 * 1024


def signed_pairs(rows_even, rows_odd):
    odd = lax.broadcasted_iota(jnp.int32, rows_even.shape, 0) % 2 == 1
    return jnp.where(odd, rows_odd, rows_even)


def mix_kernel(op_ref, listed_ref, sink_ref, peramb_ref, out_ref, left):
    products, pair_rows = listed_ref.shape[0], listed_ref.shape[1]
    eigen = sink_ref.shape[-1]
    n_cols, own2 = out_ref.shape[0], out_ref.shape[3]

    @pl.when(pl.program_id(0) == 0)
    def _():
        for k in range(products):
            op = op_ref[k, 0]
            chosen = lax.broadcasted_iota(jnp.int32, (pair_rows, eigen), 1) == listed_ref[k]
            onehot = jnp.where(chosen, 1.0, 0.0).astype(jnp.bfloat16)
            real = jnp.dot(onehot, sink_ref[0, op, 0], preferred_element_type=jnp.float32)
            imag = jnp.dot(onehot, sink_ref[0, op, 1], preferred_element_type=jnp.float32)
            rows = pl.ds(k * pair_rows, pair_rows)
            left[rows, 0:eigen] = signed_pairs(real, imag).astype(jnp.bfloat16)
            left[rows, eigen : 2 * eigen] = signed_pairs(-imag, real).astype(jnp.bfloat16)

    for k in range(products):
        rows = pl.ds(k * pair_rows, pair_rows)
        mixed = jnp.dot(
            left[rows, 0:eigen], peramb_ref[0, 0], preferred_element_type=jnp.float32
        ) + jnp.dot(
            left[rows, eigen : 2 * eigen], peramb_ref[0, 1], preferred_element_type=jnp.float32
        )
        mixed = mixed.astype(jnp.bfloat16)
        for d in range(n_cols):
            out_ref[d, k, 0] = mixed[d * own2 : (d + 1) * own2]


def mix(op_index, listed2, sink_ops, peramb, n_cols):
    products, pair_rows = listed2.shape[0], listed2.shape[1]
    eigen = sink_ops.shape[-1]
    local_cols = peramb.shape[3]
    own2 = pair_rows // n_cols
    return pl.pallas_call(
        mix_kernel,
        grid_spec=pltpu.PrefetchScalarGridSpec(
            num_scalar_prefetch=1,
            grid=(NS,),
            in_specs=[
                pl.BlockSpec(listed2.shape, lambda s, op: (0, 0, 0)),
                pl.BlockSpec(sink_ops.shape, lambda s, op: (0, 0, 0, 0, 0)),
                pl.BlockSpec((1, 2, eigen, local_cols), lambda s, op: (0, 0, s, 0)),
            ],
            out_specs=pl.BlockSpec(
                (n_cols, products, 1, own2, local_cols), lambda s, op: (0, 0, s, 0, 0)
            ),
            scratch_shapes=[pltpu.VMEM((products * pair_rows, 2 * eigen), jnp.bfloat16)],
        ),
        out_shape=jax.ShapeDtypeStruct((n_cols, products, NS, own2, local_cols), jnp.bfloat16),
        compiler_params=pltpu.CompilerParams(vmem_limit_bytes=VMEM_LIMIT),
        cost_estimate=pl.CostEstimate(
            flops=2 * NS * products * pair_rows * 2 * eigen * local_cols,
            bytes_accessed=2 * (peramb.size + sink_ops.size),
            transcendentals=0,
        ),
        name="mix",
    )(op_index, listed2, sink_ops, peramb)


def contract_kernel(n_pieces, base_ref, pos_ref, x_ref, *refs):
    pieces, out_ref, right = refs[:n_pieces], refs[n_pieces], refs[n_pieces + 1]
    n_cols, own2, local_cols = x_ref.shape[0], x_ref.shape[3], x_ref.shape[4]
    eigen = pos_ref.shape[1]
    step = min(256, eigen)
    rows = NS * own2
    for v in range(0, eigen, step):
        pos = pos_ref[0, v : v + step, :]
        total = jnp.zeros((step, 2 * eigen), jnp.float32)
        for n in range(0, n_pieces, 2):
            some = range(n, min(n + 2, n_pieces))
            chosen = [
                lax.broadcasted_iota(jnp.int32, (step, pieces[m].shape[0]), 1) == pos - base_ref[m]
                for m in some
            ]
            onehot = jnp.concatenate([jnp.where(c, 1.0, 0.0) for c in chosen], axis=1)
            table = jnp.concatenate([pieces[m][...] for m in some], axis=0)
            total += jnp.dot(
                onehot.astype(jnp.bfloat16), table, preferred_element_type=jnp.float32
            )
        total = total.astype(jnp.bfloat16)
        right[v : v + step] = total[:, :eigen]
        right[eigen + v : eigen + v + step] = total[:, eigen:]
    per_time = eigen // local_cols
    for t in range(n_cols // per_time):
        parts = [
            x_ref[j, 0].reshape(rows, local_cols) for j in range(t * per_time, (t + 1) * per_time)
        ]
        x = parts[0] if per_time == 1 else jnp.concatenate(parts, axis=1)
        wide = x.astype(jnp.float32)
        turned = signed_pairs(-pltpu.roll(wide, rows - 1, 0), pltpu.roll(wide, 1, 0))
        both = jnp.concatenate([x, turned.astype(jnp.bfloat16)], axis=1)
        result = jnp.dot(both, right[...], preferred_element_type=jnp.float32)
        result = result.astype(jnp.bfloat16).reshape(NS, own2 // 2, 2, eigen)
        out_ref[0, :, :, :, t * eigen : (t + 1) * eigen] = result


def contract(bases, pos, regrouped, pieces):
    n_cols, products, _, own2, local_cols = regrouped.shape
    eigen = pos.shape[1]
    order = n_cols * local_cols
    table_rows = sum(piece.shape[0] for piece in pieces)
    return pl.pallas_call(
        functools.partial(contract_kernel, len(pieces)),
        grid_spec=pltpu.PrefetchScalarGridSpec(
            num_scalar_prefetch=1,
            grid=(products,),
            in_specs=[
                pl.BlockSpec((1, eigen, 1), lambda k, base: (k, 0, 0)),
                pl.BlockSpec(
                    (n_cols, 1, NS, own2, local_cols), lambda k, base: (0, k, 0, 0, 0)
                ),
            ]
            + [pl.BlockSpec(piece.shape, lambda k, base: (0, 0)) for piece in pieces],
            out_specs=pl.BlockSpec(
                (1, NS, own2 // 2, 2, order), lambda k, base: (k, 0, 0, 0, 0)
            ),
            scratch_shapes=[pltpu.VMEM((2 * eigen, eigen), jnp.bfloat16)],
        ),
        out_shape=jax.ShapeDtypeStruct((products, NS, own2 // 2, 2, order), jnp.bfloat16),
        compiler_params=pltpu.CompilerParams(vmem_limit_bytes=VMEM_LIMIT),
        cost_estimate=pl.CostEstimate(
            flops=2 * products * eigen * 2 * eigen * (table_rows + NS * own2 * order // eigen),
            bytes_accessed=4 * regrouped.size,
            transcendentals=0,
        ),
        name="contract",
    )(bases, pos, regrouped, *pieces)


def gather_table(op_table, n_pair, n_cols):
    rows, eigen = op_table.shape[0], op_table.shape[2]
    me = lax.axis_index("tpair")
    if n_cols % 2 or n_pair % 2 or n_pair > 16 or rows % 32:
        own = jnp.concatenate([op_table[:, 0], op_table[:, 1]], axis=1)
        return [lax.all_gather(own, "tpair", axis=0, tiled=True)], jnp.zeros((1,), jnp.int32)
    half = rows // 2
    side = lax.axis_index("col") % 2
    own = lax.dynamic_slice_in_dim(op_table, side * half, half, 0)
    own = jnp.concatenate([own[:, 0], own[:, 1]], axis=1)
    outer = n_pair // 2

    def swap_inner(piece):
        return lax.ppermute(piece, "tpair", [(i, i ^ 1) for i in range(n_pair)])

    def swap_side(piece):
        return lax.ppermute(piece, "col", [(i, i ^ 1) for i in range(n_cols)])

    held, places = [own], [me]
    for shift in range(1, outer):
        moves = [(i, (i + 2 * shift) % n_pair) for i in range(n_pair)]
        held.append(lax.ppermute(own, "tpair", moves))
        places.append((me + n_pair - 2 * shift) % n_pair)
    held += [swap_inner(piece) for piece in held]
    places += [place ^ 1 for place in places]
    pieces, bases = [], []
    for piece, place in zip(held, places):
        pieces += [piece, swap_side(piece)]
        bases += [place * rows + side * half, place * rows + (1 - side) * half]
    return pieces, jnp.stack(bases).astype(jnp.int32)


def per_device(peramb, sink_ops, op_table, row_slot, pair_source, op_index, listed_rows):
    n_cols = lax.axis_size("col")
    n_pair = lax.axis_size("tpair")
    eigen = op_table.shape[2]
    nops = sink_ops.shape[1]
    products = op_index.shape[0]
    pieces, bases = gather_table(op_table, n_pair, n_cols)
    listed2 = jnp.repeat(listed_rows, 2, axis=1)[:, :, None]
    mixed = mix(op_index, listed2, sink_ops, peramb, n_cols)
    regrouped = lax.all_to_all(mixed, "col", split_axis=0, concat_axis=0, tiled=True)
    pos = jnp.stack(
        [
            lax.dynamic_slice_in_dim(
                row_slot, (pair_source[0] * nops + op_index[k, 1]) * eigen, eigen
            )
            for k in range(products)
        ]
    )[:, :, None]
    return contract(bases, pos, regrouped, pieces)


def solution(mesh):
    in_specs = (
        P("tpair", None, None, "col"),
        P("tpair", None, None, None, None),
        P("tpair", None, None),
        P(),
        P("tpair"),
        P("tpair", None),
        P("tpair", None),
    )
    out_specs = P("tpair", None, "col", None, None)
    return jax.shard_map(
        per_device, mesh=mesh, in_specs=in_specs, out_specs=out_specs, check_vma=False
    )
```

time: 115 us -> 77.6 us (0.67)
  the two profiles are of different devices: /device:TPU:0 before, /device:TPU:31 now
where the time goes in v1:
time: 77.6 us; the launch traced here: 77.2 us
  waiting for transfers between devices  34.1 us (44%)
  Pallas kernels  19.3 us (25%)
  starting transfers between devices  16 us (21%)
  local copies, waits for them, and re-layouts  5.79 us (7%)
  between operations  1.99 us (3%)
    ppermute x3, waiting for transfers between devices, gather_table(): held.append(lax.ppermute(own, 'tpair', moves))  20.2 us
    ppermute x4, waiting for transfers between devices, swap_inner(): return lax.ppermute(piece, 'tpair', [(i, i ^ 1) for i in range(n_pair)])  13.9 us
    pallas_call x1, Pallas kernels, contract(): pl.pallas_call(functools.partial(contract_kernel, len(pieces)), grid_spec...  11.3 us
    pallas_call x1, Pallas kernels, mix(): pl.pallas_call(mix_kernel, grid_spec=pltpu.PrefetchScalarGridSpec(num_sca...  8.01 us
    ppermute x8, starting transfers between devices, swap_side(): return lax.ppermute(piece, 'col', [(i, i ^ 1) for i in range(n_cols)])  7.88 us
    all_to_all x1, starting transfers between devices, per_device(): lax.all_to_all(mixed, 'col', split_axis=0, concat_axis=0, tiled=True)  4.53 us
    ppermute x4, starting transfers between devices, swap_inner(): return lax.ppermute(piece, 'tpair', [(i, i ^ 1) for i in range(n_pair)])  2 us
    ppermute x3, starting transfers between devices, gather_table(): held.append(lax.ppermute(own, 'tpair', moves))  1.57 us
  transfers between devices with their start and end apart: 16, of which 5 were waited for; matrix products, arithmetic and copies ran while one was open for 4% of the time, Pallas kernels for 0%

profile of v1, /device:TPU:31, one launch (start us, length us, event | category | flops | bytes accessed | tf_op | source)
XLA Modules:
  0.0 77.2 jit_solution(3945633508992685661)
XLA Ops:
  0.0 0.8 broadcast_in_dim.7
  0.8 0.8 %broadcast_in_dim_reshape.4.listed_ref = s32[2,256,1]{2,1,0:T(8,128)} reshape(s32[2,128,2]{2,1,0:T(8,128)S(1)} %broadcast_in_dim.7) | data formatting | bytes 4096 | tf_op jit(solution)/shard_map/broadcast_in_dim;reshape | solution.py:188
  1.6 8.0 %mix.1 = bf16[4,2,4,64,512]{4,3,2,1,0:T(8,128)(2,1)} custom-call(s32[2,2]{1,0:T(2,128)} %op_ref.1, s32[2,256,1]{2,1,0:T(8,128)} %broadcast_in_dim_reshape.4.listed_ref, bf16[1,2,2,512,512]{4,3,2,1,0:T(8,128)(2,1)} %sink_ref.1, bf16[1,2,2048,512]{3,2,1,0:T(8,128)(2,1)} %peramb_ref.1), custom_call_target="tpu_custom_call" | custom-call | flops 2147483648 | bytes 6291456 | tf_op jit(solution)/shard_map/mix/pallas_call | solution.py:53
  9.6 4.5 %all-to-all-start = ((bf16[4,2,4,64,512]{4,3,2,1,0:T(8,128)(2,1)}), bf16[4,2,4,64,512]{4,3,2,1,0:T(8,128)(2,1)S(1)}, u32[]{:S(2)}, u32[]{:S(2)}) async-start(bf16[4,2,4,64,512]{4,3,2,1,0:T(8,128)(2,1)} %mix.1), calls=%async_computation | async-start | bytes 4194304 | tf_op jit(solution)/shard_map/all_to_all | solution.py:190
  14.1 0.4 constant_dynamic-slice_fusion
  14.7 0.1 collective-permute-start.1
  14.7 1.3 %collective-permute-start.3 = (bf16[128,1024]{1,0:T(8,128)(2,1)S(1)}, bf16[128,1024]{1,0:T(8,128)(2,1)S(1)}, u32[]{:S(2)}, u32[]{:S(2)}) collective-permute-start(bf16[128,1024]{1,0:T(8,128)(2,1)S(1)} %pad_maximum_fusion.refs_0_), channel_id=1, source_target_pairs={{0,16},{4,20},{8,24},{12,28},{16,0},{20,4},{24,8},{28,12},{1,17},{... | collective-permute-start | bytes 786440 | tf_op jit(solution)/shard_map/ppermute | solution.py:170
  16.1 0.9 %collective-permute-start = (bf16[128,1024]{1,0:T(8,128)(2,1)S(1)}, bf16[128,1024]{1,0:T(8,128)(2,1)S(1)}, u32[]{:S(2)}, u32[]{:S(2)}) collective-permute-start(bf16[128,1024]{1,0:T(8,128)(2,1)S(1)} %pad_maximum_fusion.refs_0_), channel_id=1, source_target_pairs={{0,1},{1,0},{2,3},{3,2},{4,5},{5,4},{6,7},{7,6},{8,9},{9,8},{10,11... | collective-permute-start | bytes 786440 | tf_op jit(solution)/shard_map/ppermute | solution.py:165
  17.0 0.2 collective-permute-start.5
  17.2 0.3 collective-permute-start.7
  17.4 4.9 %collective-permute-done.1.refs_2_ = bf16[128,1024]{1,0:T(8,128)(2,1)S(1)} collective-permute-done((bf16[128,1024]{1,0:T(8,128)(2,1)S(1)}, bf16[128,1024]{1,0:T(8,128)(2,1)S(1)}, u32[]{:S(2)}, u32[]{:S(2)}) %collective-permute-start.1) | collective-permute-done | bytes 262176 | tf_op jit(solution)/shard_map/ppermute | solution.py:170
  22.3 1.3 %collective-permute-start.2 = (bf16[128,1024]{1,0:T(8,128)(2,1)S(1)}, bf16[128,1024]{1,0:T(8,128)(2,1)S(1)}, u32[]{:S(2)}, u32[]{:S(2)}) collective-permute-start(bf16[128,1024]{1,0:T(8,128)(2,1)S(1)} %collective-permute-done.1.refs_2_), channel_id=1, source_target_pairs={{0,1},{1,0},{2,3},{3,2},{4,5},{5,4},{6,7},{7,6},{8,9},{9,8},{10,11... | collective-permute-start | bytes 786440 | tf_op jit(solution)/shard_map/ppermute | solution.py:165
  23.7 15.3 %collective-permute-done.3.refs_4_ = bf16[128,1024]{1,0:T(8,128)(2,1)S(1)} collective-permute-done((bf16[128,1024]{1,0:T(8,128)(2,1)S(1)}, bf16[128,1024]{1,0:T(8,128)(2,1)S(1)}, u32[]{:S(2)}, u32[]{:S(2)}) %collective-permute-start.3) | collective-permute-done | bytes 262176 | tf_op jit(solution)/shard_map/ppermute | solution.py:170
  39.0 1.2 %collective-permute-start.4 = (bf16[128,1024]{1,0:T(8,128)(2,1)S(1)}, bf16[128,1024]{1,0:T(8,128)(2,1)S(1)}, u32[]{:S(2)}, u32[]{:S(2)}) collective-permute-start(bf16[128,1024]{1,0:T(8,128)(2,1)S(1)} %collective-permute-done.3.refs_4_), channel_id=1, source_target_pairs={{0,1},{1,0},{2,3},{3,2},{4,5},{5,4},{6,7},{7,6},{8,9},{9,8},{10,11... | collective-permute-start | bytes 786440 | tf_op jit(solution)/shard_map/ppermute | solution.py:165
  40.2 0.0 collective-permute-done.refs_1_
  40.2 0.3 collective-permute-start.9
  40.4 1.2 %collective-permute-start.11 = (bf16[128,1024]{1,0:T(8,128)(2,1)S(1)}, bf16[128,1024]{1,0:T(8,128)(2,1)}, u32[]{:S(2)}, u32[]{:S(2)}) collective-permute-start(bf16[128,1024]{1,0:T(8,128)(2,1)S(1)} %collective-permute-done.3.refs_4_), channel_id=1, source_target_pairs={{0,4},{4,0},{8,12},{12,8},{16,20},{20,16},{24,28},{28,24},{1,5},{5... | collective-permute-start | bytes 786440 | tf_op jit(solution)/shard_map/ppermute | solution.py:162
  41.7 0.3 collective-permute-start.13
  41.9 0.9 %collective-permute-start.6 = (bf16[128,1024]{1,0:T(8,128)(2,1)}, bf16[128,1024]{1,0:T(8,128)(2,1)}, u32[]{:S(2)}, u32[]{:S(2)}) collective-permute-start(bf16[128,1024]{1,0:T(8,128)(2,1)} %collective-permute-done.5.refs_6_), channel_id=1, source_target_pairs={{0,1},{1,0},{2,3},{3,2},{4,5},{5,4},{6,7},{7,6},{8,9},{9,8},{10,11... | collective-permute-start | bytes 786440 | tf_op jit(solution)/shard_map/ppermute | solution.py:165
  42.8 0.1 collective-permute-start.8
  42.9 5.2 %collective-permute-done.9.refs_10_ = bf16[128,1024]{1,0:T(8,128)(2,1)} collective-permute-done((bf16[128,1024]{1,0:T(8,128)(2,1)S(1)}, bf16[128,1024]{1,0:T(8,128)(2,1)}, u32[]{:S(2)}, u32[]{:S(2)}) %collective-permute-start.9) | collective-permute-done | bytes 262176 | tf_op jit(solution)/shard_map/ppermute | solution.py:162
  48.2 1.3 %collective-permute-start.10 = (bf16[128,1024]{1,0:T(8,128)(2,1)}, bf16[128,1024]{1,0:T(8,128)(2,1)}, u32[]{:S(2)}, u32[]{:S(2)}) collective-permute-start(bf16[128,1024]{1,0:T(8,128)(2,1)} %collective-permute-done.9.refs_10_), channel_id=1, source_target_pairs={{0,1},{1,0},{2,3},{3,2},{4,5},{5,4},{6,7},{7,6},{8,9},{9,8},{10,11... | collective-permute-start | bytes 786440 | tf_op jit(solution)/shard_map/ppermute | solution.py:165
  49.5 4.3 %collective-permute-done.11.refs_12_ = bf16[128,1024]{1,0:T(8,128)(2,1)} collective-permute-done((bf16[128,1024]{1,0:T(8,128)(2,1)S(1)}, bf16[128,1024]{1,0:T(8,128)(2,1)}, u32[]{:S(2)}, u32[]{:S(2)}) %collective-permute-start.11) | collective-permute-done | bytes 262176 | tf_op jit(solution)/shard_map/ppermute | solution.py:162
  53.8 1.3 %collective-permute-start.12 = (bf16[128,1024]{1,0:T(8,128)(2,1)}, bf16[128,1024]{1,0:T(8,128)(2,1)}, u32[]{:S(2)}, u32[]{:S(2)}) collective-permute-start(bf16[128,1024]{1,0:T(8,128)(2,1)} %collective-permute-done.11.refs_12_), channel_id=1, source_target_pairs={{0,1},{1,0},{2,3},{3,2},{4,5},{5,4},{6,7},{7,6},{8,9},{9,8},{10,11... | collective-permute-start | bytes 786440 | tf_op jit(solution)/shard_map/ppermute | solution.py:165
  55.1 4.3 %collective-permute-done.13.refs_14_ = bf16[128,1024]{1,0:T(8,128)(2,1)} collective-permute-done((bf16[128,1024]{1,0:T(8,128)(2,1)}, bf16[128,1024]{1,0:T(8,128)(2,1)}, u32[]{:S(2)}, u32[]{:S(2)}) %collective-permute-start.13) | collective-permute-done | bytes 262176 | tf_op jit(solution)/shard_map/ppermute | solution.py:162
  59.4 0.8 %collective-permute-start.14 = (bf16[128,1024]{1,0:T(8,128)(2,1)}, bf16[128,1024]{1,0:T(8,128)(2,1)}, u32[]{:S(2)}, u32[]{:S(2)}) collective-permute-start(bf16[128,1024]{1,0:T(8,128)(2,1)} %collective-permute-done.13.refs_14_), channel_id=1, source_target_pairs={{0,1},{1,0},{2,3},{3,2},{4,5},{5,4},{6,7},{7,6},{8,9},{9,8},{10,11... | collective-permute-start | bytes 786440 | tf_op jit(solution)/shard_map/ppermute | solution.py:165
  60.3 0.6 fusion.1
  62.8 0.1 fusion
  62.8 1.0 %copy.11.pos_ref = s32[2,512,1]{2,1,0:T(8,128)} copy(s32[2,512,1]{1,0,2:T(2,128)S(1)} %add_bitcast_fusion) | data formatting | bytes 8192 | tf_op jit(solution)/shard_map/broadcast_in_dim | solution.py:191
  63.9 0.6 stack.76.base_ref
  64.6 1.3 %copy-done = bf16[4,2,4,64,512]{4,3,2,1,0:T(8,128)(2,1)} copy-done((bf16[4,2,4,64,512]{4,3,2,1,0:T(8,128)(2,1)}, bf16[4,2,4,64,512]{4,3,2,1,0:T(8,128)(2,1)S(1)}, u32[]{:S(2)}) %copy-start) | copy-done | bytes 2097176
  65.9 11.3 %contract.1 = bf16[2,4,32,2,2048]{4,3,2,1,0:T(2,128)(2,1)} custom-call(s32[16]{0:T(128)} %stack.76.base_ref, s32[2,512,1]{2,1,0:T(8,128)} %copy.11.pos_ref, bf16[4,2,4,64,512]{4,3,2,1,0:T(8,128)(2,1)} %copy-done, bf16[128,1024]{1,0:T(8,128)(2,1)} %copy-done.2, bf16[128,1024]{1,0:T(8,128)(2,1)} %copy-done.7, bf16[128,1024]{1,0:T(8,128)(2,1)} %copy-done.5, ...), custom_call_target="tpu_custom_call" | custom-call | flops 6442450944 | bytes 4194304 | tf_op jit(solution)/shard_map/contract/pallas_call | solution.py:121
  (32 shorter events, 0.1 us)
Async XLA Ops:
  9.6 4.5 %copy-start.1 = (bf16[256,2,512]{2,1,0:T(2,128)(2,1)S(1)}, bf16[256,2,512]{2,1,0:T(2,128)(2,1)}, u32[]{:S(2)}) copy-start(bf16[256,2,512]{2,1,0:T(2,128)(2,1)} %param.9) | copy-start | bytes 1572868
  9.6 54.9 %all-to-all-start = ((bf16[4,2,4,64,512]{4,3,2,1,0:T(8,128)(2,1)}), bf16[4,2,4,64,512]{4,3,2,1,0:T(8,128)(2,1)S(1)}, u32[]{:S(2)}, u32[]{:S(2)}) async-start(bf16[4,2,4,64,512]{4,3,2,1,0:T(8,128)(2,1)} %mix.1), calls=%async_computation | async-start | bytes 4194304 | tf_op jit(solution)/shard_map/all_to_all | solution.py:190
  14.1 46.1 %copy-start.3 = (s32[2,2]{1,0:T(2,128)S(1)}, s32[2,2]{1,0:T(2,128)}, u32[]{:S(2)}) copy-start(s32[2,2]{1,0:T(2,128)} %op_ref.1) | copy-start | bytes 52
  14.1 48.6 %copy-start.4 = (s32[2048]{0:T(1024)S(1)}, s32[2048]{0:T(1024)}, u32[]{:S(2)}) copy-start(s32[2048]{0:T(1024)} %param.10) | copy-start | bytes 24580
  14.6 49.9 %copy-start.2 = (bf16[128,1024]{1,0:T(8,128)(2,1)}, bf16[128,1024]{1,0:T(8,128)(2,1)S(1)}, u32[]{:S(2)}) copy-start(bf16[128,1024]{1,0:T(8,128)(2,1)S(1)} %pad_maximum_fusion.refs_0_) | copy-start | bytes 786436
  14.7 7.7 %collective-permute-start.1 = (bf16[128,1024]{1,0:T(8,128)(2,1)S(1)}, bf16[128,1024]{1,0:T(8,128)(2,1)S(1)}, u32[]{:S(2)}, u32[]{:S(2)}) collective-permute-start(bf16[128,1024]{1,0:T(8,128)(2,1)S(1)} %pad_maximum_fusion.refs_0_), channel_id=1, source_target_pairs={{0,8},{4,12},{8,16},{12,20},{16,24},{20,28},{24,0},{28,4},{1,9},{5... | collective-permute-start | bytes 786440 | tf_op jit(solution)/shard_map/ppermute | solution.py:170
  14.7 24.3 %collective-permute-start.3 = (bf16[128,1024]{1,0:T(8,128)(2,1)S(1)}, bf16[128,1024]{1,0:T(8,128)(2,1)S(1)}, u32[]{:S(2)}, u32[]{:S(2)}) collective-permute-start(bf16[128,1024]{1,0:T(8,128)(2,1)S(1)} %pad_maximum_fusion.refs_0_), channel_id=1, source_target_pairs={{0,16},{4,20},{8,24},{12,28},{16,0},{20,4},{24,8},{28,12},{1,17},{... | collective-permute-start | bytes 786440 | tf_op jit(solution)/shard_map/ppermute | solution.py:170
  16.1 24.1 %collective-permute-start = (bf16[128,1024]{1,0:T(8,128)(2,1)S(1)}, bf16[128,1024]{1,0:T(8,128)(2,1)S(1)}, u32[]{:S(2)}, u32[]{:S(2)}) collective-permute-start(bf16[128,1024]{1,0:T(8,128)(2,1)S(1)} %pad_maximum_fusion.refs_0_), channel_id=1, source_target_pairs={{0,1},{1,0},{2,3},{3,2},{4,5},{5,4},{6,7},{7,6},{8,9},{9,8},{10,11... | collective-permute-start | bytes 786440 | tf_op jit(solution)/shard_map/ppermute | solution.py:165
  17.0 23.5 %collective-permute-start.5 = (bf16[128,1024]{1,0:T(8,128)(2,1)S(1)}, bf16[128,1024]{1,0:T(8,128)(2,1)}, u32[]{:S(2)}, u32[]{:S(2)}) collective-permute-start(bf16[128,1024]{1,0:T(8,128)(2,1)S(1)} %pad_maximum_fusion.refs_0_), channel_id=1, source_target_pairs={{0,24},{4,28},{8,0},{12,4},{16,8},{20,12},{24,16},{28,20},{1,25},{... | collective-permute-start | bytes 786440 | tf_op jit(solution)/shard_map/ppermute | solution.py:170
  17.2 24.5 %collective-permute-start.7 = (bf16[128,1024]{1,0:T(8,128)(2,1)S(1)}, bf16[128,1024]{1,0:T(8,128)(2,1)}, u32[]{:S(2)}, u32[]{:S(2)}) collective-permute-start(bf16[128,1024]{1,0:T(8,128)(2,1)S(1)} %pad_maximum_fusion.refs_0_), channel_id=1, source_target_pairs={{0,4},{4,0},{8,12},{12,8},{16,20},{20,16},{24,28},{28,24},{1,5},{5... | collective-permute-start | bytes 786440 | tf_op jit(solution)/shard_map/ppermute | solution.py:162
  22.3 42.2 %copy-start.5 = (bf16[128,1024]{1,0:T(8,128)(2,1)}, bf16[128,1024]{1,0:T(8,128)(2,1)S(1)}, u32[]{:S(2)}) copy-start(bf16[128,1024]{1,0:T(8,128)(2,1)S(1)} %collective-permute-done.1.refs_2_) | copy-start | bytes 786436
  22.3 19.6 %collective-permute-start.2 = (bf16[128,1024]{1,0:T(8,128)(2,1)S(1)}, bf16[128,1024]{1,0:T(8,128)(2,1)S(1)}, u32[]{:S(2)}, u32[]{:S(2)}) collective-permute-start(bf16[128,1024]{1,0:T(8,128)(2,1)S(1)} %collective-permute-done.1.refs_2_), channel_id=1, source_target_pairs={{0,1},{1,0},{2,3},{3,2},{4,5},{5,4},{6,7},{7,6},{8,9},{9,8},{10,11... | collective-permute-start | bytes 786440 | tf_op jit(solution)/shard_map/ppermute | solution.py:165
  39.0 25.6 %copy-start.6 = (bf16[128,1024]{1,0:T(8,128)(2,1)}, bf16[128,1024]{1,0:T(8,128)(2,1)S(1)}, u32[]{:S(2)}) copy-start(bf16[128,1024]{1,0:T(8,128)(2,1)S(1)} %collective-permute-done.3.refs_4_) | copy-start | bytes 786436
  39.0 3.9 %collective-permute-start.4 = (bf16[128,1024]{1,0:T(8,128)(2,1)S(1)}, bf16[128,1024]{1,0:T(8,128)(2,1)S(1)}, u32[]{:S(2)}, u32[]{:S(2)}) collective-permute-start(bf16[128,1024]{1,0:T(8,128)(2,1)S(1)} %collective-permute-done.3.refs_4_), channel_id=1, source_target_pairs={{0,1},{1,0},{2,3},{3,2},{4,5},{5,4},{6,7},{7,6},{8,9},{9,8},{10,11... | collective-permute-start | bytes 786440 | tf_op jit(solution)/shard_map/ppermute | solution.py:165
  40.2 24.4 %copy-start.7 = (bf16[128,1024]{1,0:T(8,128)(2,1)}, bf16[128,1024]{1,0:T(8,128)(2,1)S(1)}, u32[]{:S(2)}) copy-start(bf16[128,1024]{1,0:T(8,128)(2,1)S(1)} %collective-permute-done.refs_1_) | copy-start | bytes 786436
  40.2 8.0 %collective-permute-start.9 = (bf16[128,1024]{1,0:T(8,128)(2,1)S(1)}, bf16[128,1024]{1,0:T(8,128)(2,1)}, u32[]{:S(2)}, u32[]{:S(2)}) collective-permute-start(bf16[128,1024]{1,0:T(8,128)(2,1)S(1)} %collective-permute-done.1.refs_2_), channel_id=1, source_target_pairs={{0,4},{4,0},{8,12},{12,8},{16,20},{20,16},{24,28},{28,24},{1,5},{5... | collective-permute-start | bytes 786440 | tf_op jit(solution)/shard_map/ppermute | solution.py:162
  40.4 13.3 %collective-permute-start.11 = (bf16[128,1024]{1,0:T(8,128)(2,1)S(1)}, bf16[128,1024]{1,0:T(8,128)(2,1)}, u32[]{:S(2)}, u32[]{:S(2)}) collective-permute-start(bf16[128,1024]{1,0:T(8,128)(2,1)S(1)} %collective-permute-done.3.refs_4_), channel_id=1, source_target_pairs={{0,4},{4,0},{8,12},{12,8},{16,20},{20,16},{24,28},{28,24},{1,5},{5... | collective-permute-start | bytes 786440 | tf_op jit(solution)/shard_map/ppermute | solution.py:162
  41.7 17.7 %collective-permute-start.13 = (bf16[128,1024]{1,0:T(8,128)(2,1)}, bf16[128,1024]{1,0:T(8,128)(2,1)}, u32[]{:S(2)}, u32[]{:S(2)}) collective-permute-start(bf16[128,1024]{1,0:T(8,128)(2,1)} %collective-permute-done.5.refs_6_), channel_id=1, source_target_pairs={{0,4},{4,0},{8,12},{12,8},{16,20},{20,16},{24,28},{28,24},{1,5},{5... | collective-permute-start | bytes 786440 | tf_op jit(solution)/shard_map/ppermute | solution.py:162
  41.9 20.9 %copy-start.8 = (bf16[128,1024]{1,0:T(8,128)(2,1)}, bf16[128,1024]{1,0:T(8,128)(2,1)S(1)}, u32[]{:S(2)}) copy-start(bf16[128,1024]{1,0:T(8,128)(2,1)S(1)} %collective-permute-done.2.refs_3_) | copy-start | bytes 786436
  41.9 22.5 %collective-permute-start.6 = (bf16[128,1024]{1,0:T(8,128)(2,1)}, bf16[128,1024]{1,0:T(8,128)(2,1)}, u32[]{:S(2)}, u32[]{:S(2)}) collective-permute-start(bf16[128,1024]{1,0:T(8,128)(2,1)} %collective-permute-done.5.refs_6_), channel_id=1, source_target_pairs={{0,1},{1,0},{2,3},{3,2},{4,5},{5,4},{6,7},{7,6},{8,9},{9,8},{10,11... | collective-permute-start | bytes 786440 | tf_op jit(solution)/shard_map/ppermute | solution.py:165
  42.8 11.0 %copy-start.9 = (bf16[128,1024]{1,0:T(8,128)(2,1)}, bf16[128,1024]{1,0:T(8,128)(2,1)S(1)}, u32[]{:S(2)}) copy-start(bf16[128,1024]{1,0:T(8,128)(2,1)S(1)} %collective-permute-done.4.refs_5_) | copy-start | bytes 786436
  42.8 21.7 %collective-permute-start.8 = (bf16[128,1024]{1,0:T(8,128)(2,1)}, bf16[128,1024]{1,0:T(8,128)(2,1)}, u32[]{:S(2)}, u32[]{:S(2)}) collective-permute-start(bf16[128,1024]{1,0:T(8,128)(2,1)} %collective-permute-done.7.refs_8_), channel_id=1, source_target_pairs={{0,1},{1,0},{2,3},{3,2},{4,5},{5,4},{6,7},{7,6},{8,9},{9,8},{10,11... | collective-permute-start | bytes 786440 | tf_op jit(solution)/shard_map/ppermute | solution.py:165
  48.2 16.3 %collective-permute-start.10 = (bf16[128,1024]{1,0:T(8,128)(2,1)}, bf16[128,1024]{1,0:T(8,128)(2,1)}, u32[]{:S(2)}, u32[]{:S(2)}) collective-permute-start(bf16[128,1024]{1,0:T(8,128)(2,1)} %collective-permute-done.9.refs_10_), channel_id=1, source_target_pairs={{0,1},{1,0},{2,3},{3,2},{4,5},{5,4},{6,7},{7,6},{8,9},{9,8},{10,11... | collective-permute-start | bytes 786440 | tf_op jit(solution)/shard_map/ppermute | solution.py:165
  53.8 10.7 %collective-permute-start.12 = (bf16[128,1024]{1,0:T(8,128)(2,1)}, bf16[128,1024]{1,0:T(8,128)(2,1)}, u32[]{:S(2)}, u32[]{:S(2)}) collective-permute-start(bf16[128,1024]{1,0:T(8,128)(2,1)} %collective-permute-done.11.refs_12_), channel_id=1, source_target_pairs={{0,1},{1,0},{2,3},{3,2},{4,5},{5,4},{6,7},{7,6},{8,9},{9,8},{10,11... | collective-permute-start | bytes 786440 | tf_op jit(solution)/shard_map/ppermute | solution.py:165
  59.4 5.1 %collective-permute-start.14 = (bf16[128,1024]{1,0:T(8,128)(2,1)}, bf16[128,1024]{1,0:T(8,128)(2,1)}, u32[]{:S(2)}, u32[]{:S(2)}) collective-permute-start(bf16[128,1024]{1,0:T(8,128)(2,1)} %collective-permute-done.13.refs_14_), channel_id=1, source_target_pairs={{0,1},{1,0},{2,3},{3,2},{4,5},{5,4},{6,7},{7,6},{8,9},{9,8},{10,11... | collective-permute-start | bytes 786440 | tf_op jit(solution)/shard_map/ppermute | solution.py:165
  64.6 1.4 %copy-start = (bf16[4,2,4,64,512]{4,3,2,1,0:T(8,128)(2,1)}, bf16[4,2,4,64,512]{4,3,2,1,0:T(8,128)(2,1)S(1)}, u32[]{:S(2)}) copy-start(bf16[4,2,4,64,512]{4,3,2,1,0:T(8,128)(2,1)S(1)} %all-to-all-done.x_ref) | copy-start | bytes 6291460

commit v2 on v0

v2 whole, which is shorter than its diff:
```python
import functools

import jax
import jax.numpy as jnp
from jax import lax
from jax.experimental import pallas as pl
from jax.experimental.pallas import tpu as pltpu
from jax.sharding import PartitionSpec as P

NS = 4
LANES = 128
VMEM_LIMIT = 56 * 1024 * 1024
BF16, F32 = jnp.bfloat16, jnp.float32


def iota(shape, dim):
    return lax.broadcasted_iota(jnp.int32, shape, dim)


def dot(a, b):
    return jnp.dot(a, b, preferred_element_type=F32)


def column(row):
    wide = jnp.broadcast_to(row, (LANES, LANES)).astype(F32)
    return jnp.transpose(wide).astype(jnp.int32)


def one_hot(col, first, width):
    tiles = [
        jnp.where(col - (first + n) == iota((col.shape[0], LANES), 1), 1.0, 0.0)
        for n in range(0, width, LANES)
    ]
    return jnp.concatenate(tiles, axis=1).astype(BF16)


def mix_kernel(op_ref, listed_ref, sink_ref, peramb_ref, *refs):
    outs, left = refs[:-1], refs[-1]
    n_cols = len(outs)
    products, listed = listed_ref.shape
    eigen = sink_ref.shape[-1]
    own2 = 2 * listed // n_cols

    @pl.when(pl.program_id(0) == 0)
    def _():
        me = lax.axis_index("col")
        row = iota((2 * listed, 2 * listed), 0)
        wanted = ((row // own2) ^ me) * (own2 // 2) + (row % own2) // 2 + (row % 2) * listed
        order = jnp.where(wanted == iota((2 * listed, 2 * listed), 1), 1.0, 0.0).astype(BF16)
        for k in range(products):
            op = op_ref[k, 0]
            onehot = one_hot(column(listed_ref[k : k + 1, :]), 0, eigen)
            real = dot(onehot, sink_ref[0, op, 0])
            imag = dot(onehot, sink_ref[0, op, 1])
            top = jnp.concatenate([real, -imag], axis=1)
            bottom = jnp.concatenate([imag, real], axis=1)
            both = jnp.concatenate([top, bottom], axis=0).astype(BF16)
            rows = dot(order, both).astype(BF16)
            for j in range(n_cols):
                at = (j * products + k) * own2
                left[at : at + own2, :] = rows[j * own2 : (j + 1) * own2]

    mixed = dot(left[:, :eigen], peramb_ref[0, 0]) + dot(left[:, eigen:], peramb_ref[0, 1])
    mixed = mixed.astype(BF16)
    for j in range(n_cols):
        for k in range(products):
            at = (j * products + k) * own2
            outs[j][k, 0] = mixed[at : at + own2]


def mix(op_index, listed_rows, sink_ops, peramb, n_cols):
    products, listed = listed_rows.shape
    eigen = sink_ops.shape[-1]
    local_cols = peramb.shape[3]
    own2 = 2 * listed // n_cols
    block = jax.ShapeDtypeStruct((products, NS, own2, local_cols), BF16)
    return pl.pallas_call(
        mix_kernel,
        grid_spec=pltpu.PrefetchScalarGridSpec(
            num_scalar_prefetch=1,
            grid=(NS,),
            in_specs=[
                pl.BlockSpec(listed_rows.shape, lambda s, op: (0, 0)),
                pl.BlockSpec(sink_ops.shape, lambda s, op: (0, 0, 0, 0, 0)),
                pl.BlockSpec((1, 2, eigen, local_cols), lambda s, op: (0, 0, s, 0)),
            ],
            out_specs=[
                pl.BlockSpec((products, 1, own2, local_cols), lambda s, op: (0, s, 0, 0))
            ]
            * n_cols,
            scratch_shapes=[pltpu.VMEM((products * 2 * listed, 2 * eigen), BF16)],
        ),
        out_shape=[block] * n_cols,
        compiler_params=pltpu.CompilerParams(vmem_limit_bytes=VMEM_LIMIT),
        cost_estimate=pl.CostEstimate(flops=1000, bytes_accessed=1000, transcendentals=0),
        name="mix",
    )(op_index, listed_rows, sink_ops, peramb)


def add_pieces(places, scalars_ref, slot_ref, pieces, products, eigen):
    source_ref, op_ref = scalars_ref
    blocks = eigen // LANES
    nops = slot_ref.shape[0] // blocks // 2
    pair, side = lax.axis_index("tpair"), lax.axis_index("col") % 2
    cols = []
    for k in range(products):
        op = source_ref[0] * nops + op_ref[k, 1]
        cols += [
            column(slot_ref[pl.ds(op * blocks + b, 1), :]) for b in range(blocks)
        ]
    col = jnp.concatenate(cols, axis=0)
    tiles, tables = [], []
    for place, piece in zip(places, pieces):
        height = piece.shape[0]
        first = place
        if isinstance(place, tuple):
            first = (2 * (pair ^ place[0]) + (side ^ place[1])) * height
        tiles.append(one_hot(col, first, height))
        tables.append(piece[...])
    return dot(jnp.concatenate(tiles, axis=1), jnp.concatenate(tables, axis=0))


def assemble_kernel(places, source_ref, op_ref, slot_ref, *refs):
    pieces, out_ref = refs[:-1], refs[-1]
    products, eigen = out_ref.shape[0], out_ref.shape[2]
    total = add_pieces(places, (source_ref, op_ref), slot_ref, pieces, products, eigen)
    total = total.astype(BF16)
    for k in range(products):
        rows = slice(k * eigen, (k + 1) * eigen)
        out_ref[k, :eigen] = total[rows, :eigen]
        out_ref[k, eigen:] = total[rows, eigen:]


def assemble(places, pieces, source, op_index, slots, eigen):
    products = op_index.shape[0]
    vmem = pl.BlockSpec(memory_space=pltpu.VMEM)
    smem = pl.BlockSpec(memory_space=pltpu.SMEM)
    return pl.pallas_call(
        functools.partial(assemble_kernel, places),
        in_specs=[smem, smem] + [vmem] * (1 + len(pieces)),
        out_specs=vmem,
        out_shape=jax.ShapeDtypeStruct((products, 2 * eigen, eigen), BF16),
        compiler_params=pltpu.CompilerParams(vmem_limit_bytes=VMEM_LIMIT),
        cost_estimate=pl.CostEstimate(flops=1000, bytes_accessed=1000, transcendentals=0),
        name="assemble",
    )(source, op_index, slots, *pieces)


def contract_kernel(places, n_cols, source_ref, op_ref, slot_ref, partial_ref, *refs):
    n_pieces = len(places)
    pieces, blocks = refs[:n_pieces], refs[n_pieces : n_pieces + n_cols]
    out_ref, right = refs[-2], refs[-1]
    own2, local_cols = blocks[0].shape[2], blocks[0].shape[3]
    products, eigen = right.shape[0], right.shape[2]
    rows = NS * own2
    k = pl.program_id(0)

    @pl.when(k == 0)
    def _():
        total = add_pieces(places, (source_ref, op_ref), slot_ref, pieces, products, eigen)
        total = total.astype(BF16)
        for p in range(products):
            some = slice(p * eigen, (p + 1) * eigen)
            right[p, :eigen] = partial_ref[p, :eigen] + total[some, :eigen]
            right[p, eigen:] = partial_ref[p, eigen:] + total[some, eigen:]

    me = lax.axis_index("col")
    per_time = eigen // local_cols
    odd = iota((rows, local_cols), 0) % 2 == 1
    for g in range(0, n_cols, per_time):
        result = None
        for j in range(g, g + per_time):
            x = blocks[j][0].reshape(rows, local_cols)
            wide = x.astype(F32)
            turned = jnp.where(odd, pltpu.roll(wide, 1, 0), -pltpu.roll(wide, rows - 1, 0))
            if per_time == 1:
                part = dot(jnp.concatenate([x, turned.astype(BF16)], axis=1), right[k])
            else:
                first = pl.multiple_of(((me ^ j) % per_time) * local_cols, local_cols)
                part = dot(x, right[k, pl.ds(first, local_cols), :])
                second = pl.multiple_of(eigen + first, local_cols)
                part += dot(turned.astype(BF16), right[k, pl.ds(second, local_cols), :])
            result = part if result is None else result + part
        result = result.astype(BF16).reshape(NS, own2 // 2, 2, eigen)
        at = pl.multiple_of(((me ^ g) // per_time) * eigen, eigen)
        out_ref[0, :, :, :, pl.ds(at, eigen)] = result


def contract(places, pieces, partial, source, op_index, slots, blocks):
    products, _, own2, local_cols = blocks[0].shape
    n_cols = len(blocks)
    eigen = partial.shape[2]
    order = n_cols * local_cols
    return pl.pallas_call(
        functools.partial(contract_kernel, places, n_cols),
        grid_spec=pltpu.PrefetchScalarGridSpec(
            num_scalar_prefetch=2,
            grid=(products,),
            in_specs=[
                pl.BlockSpec(slots.shape, lambda k, *_: (0, 0)),
                pl.BlockSpec(partial.shape, lambda k, *_: (0, 0, 0)),
            ]
            + [pl.BlockSpec(piece.shape, lambda k, *_: (0, 0)) for piece in pieces]
            + [pl.BlockSpec((1, NS, own2, local_cols), lambda k, *_: (k, 0, 0, 0))] * n_cols,
            out_specs=pl.BlockSpec(
                (1, NS, own2 // 2, 2, order), lambda k, *_: (k, 0, 0, 0, 0)
            ),
            scratch_shapes=[pltpu.VMEM((products, 2 * eigen, eigen), BF16)],
        ),
        out_shape=jax.ShapeDtypeStruct((products, NS, own2 // 2, 2, order), BF16),
        compiler_params=pltpu.CompilerParams(vmem_limit_bytes=VMEM_LIMIT),
        cost_estimate=pl.CostEstimate(
            flops=4 * products * eigen * NS * own2 * order, bytes_accessed=0, transcendentals=0
        ),
        name="contract",
    )(source, op_index, slots, partial, *pieces, *blocks)


def swap(array, axis, size, mask):
    return lax.ppermute(array, axis, [(i, i ^ mask) for i in range(size)])


def gather_table(op_table, n_pair, n_cols):
    rows = op_table.shape[0]
    if n_cols % 2 or n_pair % 2 or n_pair > 16 or rows % 32:
        own = jnp.concatenate([op_table[:, 0], op_table[:, 1]], axis=1)
        whole = lax.all_gather(own, "tpair", axis=0, tiled=True)
        half = whole.shape[0] // 2
        return [0, half], [whole[:half], whole[half:]]
    half = rows // 2
    own = lax.dynamic_slice_in_dim(op_table, lax.axis_index("col") % 2 * half, half, 0)
    own = jnp.concatenate([own[:, 0], own[:, 1]], axis=1)
    places, pieces = [], []
    for mask in range(0, n_pair, 2):
        outer = own if mask == 0 else swap(own, "tpair", n_pair, mask)
        inner = swap(outer, "tpair", n_pair, 1)
        places += [(mask, 0), (mask, 1), (mask + 1, 0), (mask + 1, 1)]
        pieces += [outer, swap(outer, "col", n_cols, 1), inner, swap(inner, "col", n_cols, 1)]
    return places, pieces


def per_device(peramb, sink_ops, op_table, row_slot, pair_source, op_index, listed_rows):
    n_cols = lax.axis_size("col")
    n_pair = lax.axis_size("tpair")
    eigen = op_table.shape[2]
    places, pieces = gather_table(op_table, n_pair, n_cols)
    blocks = mix(op_index, listed_rows, sink_ops, peramb, n_cols)
    blocks = [blocks[0]] + [swap(blocks[j], "col", n_cols, j) for j in range(1, n_cols)]
    slots = row_slot.reshape(-1, LANES)
    late = 4 if len(pieces) > 4 else 1
    partial = assemble(places[:-late], pieces[:-late], pair_source, op_index, slots, eigen)
    return contract(
        places[-late:], pieces[-late:], partial, pair_source, op_index, slots, blocks
    )


def solution(mesh):
    in_specs = (
        P("tpair", None, None, "col"),
        P("tpair", None, None, None, None),
        P("tpair", None, None),
        P(),
        P("tpair"),
        P("tpair", None),
        P("tpair", None),
    )
    out_specs = P("tpair", None, "col", None, None)
    return jax.shard_map(
        per_device, mesh=mesh, in_specs=in_specs, out_specs=out_specs, check_vma=False
    )
```

time: 115 us -> 74.3 us (0.65)
  local copies, waits for them, and re-layouts: 31.7 us -> 2.42 us
  Pallas kernels: 0 us -> 22.9 us
  waiting for transfers between devices: 53.9 us -> 32.1 us
  between operations: 14.2 us -> 0.87 us
  starting transfers between devices: 4.64 us -> 15.8 us
  matrix products: 8.13 us -> 0 us
  other arithmetic: 2.04 us -> 0.02 us
    all_gather x1 -> x0, waiting for transfers between devices: 53.2 us -> none  [per_device(): gathered = lax.all_gather(op_table, 'tpair', axis=0, tiled=True)]
    ppermute x0 -> x18, waiting for transfers between devices: none -> 32.1 us  [swap(): return lax.ppermute(array, axis, [(i, i ^ mask) for i in range(size)])]
    pallas_call x0 -> x3, Pallas kernels: none -> 22.9 us  [the longest x1 8.14 us: mix(): pl.pallas_call(mix_kernel, grid_spec=pltpu.PrefetchScalarGridSpec(num_sca...]
    gather x6 -> x0, local copies, waits for them, and re-layouts: 16.6 us -> none  [the longest x2 8.39 us: per_device(): right = gathered[right_pos]]
    ppermute x0 -> x18, starting transfers between devices: none -> 15.8 us  [swap(): return lax.ppermute(array, axis, [(i, i ^ mask) for i in range(size)])]
    dot_general x2 -> x0, matrix products: 8.13 us -> none  [the longest x1 5.77 us: per_device(): jnp.einsum('pjsitv,pjvow->psiotw', split, right_block, preferred_element_...]
    convert_element_type x3 -> x0, local copies, waits for them, and re-layouts: 6.78 us -> none  [the longest x2 3.84 us: per_device(): result.reshape(products, spins, own_rows, 2, order_full)]
    unnamed x15 -> x38, local copies, waits for them, and re-layouts: 6.66 us -> 0.93 us
  transfers between devices with their start and end apart: 2 -> 18, of which waited for: 1 -> 6; matrix products, arithmetic and copies ran while one was open for 26% -> 0% of each run, Pallas kernels for 0% -> 20%
where the time goes in v2:
time: 74.3 us; the launch traced here: 74.1 us
  waiting for transfers between devices  32.1 us (43%)
  Pallas kernels  22.9 us (31%)
  starting transfers between devices  15.8 us (21%)
  local copies, waits for them, and re-layouts  2.42 us (3%)
  between operations  0.87 us (1%)
    ppermute x18, waiting for transfers between devices, swap(): return lax.ppermute(array, axis, [(i, i ^ mask) for i in range(size)])  32.1 us
    ppermute x18, starting transfers between devices, swap(): return lax.ppermute(array, axis, [(i, i ^ mask) for i in range(size)])  15.8 us
    pallas_call x1, Pallas kernels, mix(): pl.pallas_call(mix_kernel, grid_spec=pltpu.PrefetchScalarGridSpec(num_sca...  8.14 us
    pallas_call x1, Pallas kernels, contract(): pl.pallas_call(functools.partial(contract_kernel, places, n_cols), grid_s...  8.07 us
    pallas_call x1, Pallas kernels, assemble(): pl.pallas_call(functools.partial(assemble_kernel, places), in_specs=[smem...  6.68 us
  transfers between devices with their start and end apart: 18, of which 6 were waited for; matrix products, arithmetic and copies ran while one was open for 0% of the time, Pallas kernels for 20%

profile of v2, /device:TPU:0, one launch (start us, length us, event | category | flops | bytes accessed | tf_op | source)
XLA Modules:
  0.0 74.1 jit_solution(7059573031070630662)
XLA Ops:
  0.0 1.5 %constant_dynamic-slice_fusion = (bf16[128,1,512]{2,1,0:T(2,128)(2,1)S(1)}, bf16[128,1,512]{2,1,0:T(2,128)(2,1)S(1)}) fusion(bf16[256,2,512]{2,1,0:T(2,128)(2,1)} %param.9, s32[]{:T(128)S(6)} %select_n.11, s32[]{:T(128)S(6)} %add.9), kind=kLoop, calls=%fused_computation.3 | loop fusion | bytes 524296 | tf_op jit(solution)/shard_map/slice | solution.py:232
  1.5 5.1 %collective-permute-start.11 = (bf16[128,1024]{1,0:T(8,128)(2,1)S(1)}, bf16[128,1024]{1,0:T(8,128)(2,1)S(1)}, u32[]{:S(2)}, u32[]{:S(2)}) collective-permute-start(bf16[128,1024]{1,0:T(8,128)(2,1)S(1)} %pad_maximum_fusion.refs_0_), channel_id=1, source_target_pairs={{0,24},{4,28},{8,16},{12,20},{16,8},{20,12},{24,0},{28,4},{1,25},{... | collective-permute-start | bytes 786440 | tf_op jit(solution)/shard_map/ppermute | solution.py:220
  6.7 0.0 collective-permute-start.7
  6.7 0.6 collective-permute-start.3
  7.3 1.6 %collective-permute-start.1 = (bf16[128,1024]{1,0:T(8,128)(2,1)S(1)}, bf16[128,1024]{1,0:T(8,128)(2,1)S(1)}, u32[]{:S(2)}, u32[]{:S(2)}) collective-permute-start(bf16[128,1024]{1,0:T(8,128)(2,1)S(1)} %pad_maximum_fusion.refs_0_), channel_id=1, source_target_pairs={{0,4},{4,0},{8,12},{12,8},{16,20},{20,16},{24,28},{28,24},{1,5},{5... | collective-permute-start | bytes 786440 | tf_op jit(solution)/shard_map/ppermute | solution.py:220
  8.9 0.0 collective-permute-start
  8.9 5.0 %collective-permute-done.11.refs_0_ = bf16[128,1024]{1,0:T(8,128)(2,1)S(1)} collective-permute-done((bf16[128,1024]{1,0:T(8,128)(2,1)S(1)}, bf16[128,1024]{1,0:T(8,128)(2,1)S(1)}, u32[]{:S(2)}, u32[]{:S(2)}) %collective-permute-start.11) | collective-permute-done | bytes 262176 | tf_op jit(solution)/shard_map/ppermute | solution.py:220
  13.9 1.7 %collective-permute-start.13 = (bf16[128,1024]{1,0:T(8,128)(2,1)S(1)}, bf16[128,1024]{1,0:T(8,128)(2,1)S(1)}, u32[]{:S(2)}, u32[]{:S(2)}) collective-permute-start(bf16[128,1024]{1,0:T(8,128)(2,1)S(1)} %collective-permute-done.11.refs_0_), channel_id=1, source_target_pairs={{0,4},{4,0},{8,12},{12,8},{16,20},{20,16},{24,28},{28,24},{1,5},{5... | collective-permute-start | bytes 786440 | tf_op jit(solution)/shard_map/ppermute | solution.py:220
  15.6 13.3 %collective-permute-done.7.refs_8_ = bf16[128,1024]{1,0:T(8,128)(2,1)S(1)} collective-permute-done((bf16[128,1024]{1,0:T(8,128)(2,1)S(1)}, bf16[128,1024]{1,0:T(8,128)(2,1)S(1)}, u32[]{:S(2)}, u32[]{:S(2)}) %collective-permute-start.7) | collective-permute-done | bytes 262176 | tf_op jit(solution)/shard_map/ppermute | solution.py:220
  29.0 1.5 %collective-permute-start.9 = (bf16[128,1024]{1,0:T(8,128)(2,1)S(1)}, bf16[128,1024]{1,0:T(8,128)(2,1)S(1)}, u32[]{:S(2)}, u32[]{:S(2)}) collective-permute-start(bf16[128,1024]{1,0:T(8,128)(2,1)S(1)} %collective-permute-done.7.refs_8_), channel_id=1, source_target_pairs={{0,4},{4,0},{8,12},{12,8},{16,20},{20,16},{24,28},{28,24},{1,5},{5... | collective-permute-start | bytes 786440 | tf_op jit(solution)/shard_map/ppermute | solution.py:220
  30.5 0.0 collective-permute-done.3.refs_4_
  30.5 0.0 collective-permute-done.1.refs_2_
  30.5 0.6 collective-permute-start.5
  31.1 0.2 collective-permute-start.4
  31.3 0.0 collective-permute-done.13.refs_2_
  31.3 0.4 collective-permute-start.2
  31.6 8.1 %mix.1 = (bf16[2,4,64,512]{3,2,1,0:T(8,128)(2,1)}, bf16[2,4,64,512]{3,2,1,0:T(8,128)(2,1)}, bf16[2,4,64,512]{3,2,1,0:T(8,128)(2,1)}, bf16[2,4,64,512]{3,2,1,0:T(8,128)(2,1)}) custom-call(s32[2,2]{1,0:T(2,128)} %op_ref.5, s32[2,128]{1,0:T(2,128)} %listed_ref.1, bf16[1,2,2,512,512]{4,3,2,1,0:T(8,128)(2,1)} %sink_ref.1, bf16[1,2,2048,512]{3,2,1,0:T(8,128)(2,1)} %peramb_ref.1), custom_call_target="tpu_custom_call" | custom-call | flops 1000 | bytes 1000 | tf_op jit(solution)/shard_map/mix/pallas_call | solution.py:77
  39.8 0.2 collective-permute-start.15
  40.0 0.0 collective-permute-done.8.refs_9_
  40.0 1.5 %collective-permute-start.16 = (bf16[2,4,64,512]{3,2,1,0:T(8,128)(2,1)}, bf16[2,4,64,512]{3,2,1,0:T(8,128)(2,1)S(1)}, u32[]{:S(2)}, u32[]{:S(2)}) collective-permute-start(bf16[2,4,64,512]{3,2,1,0:T(8,128)(2,1)} %get-tuple-element.11), channel_id=1, source_target_pairs={{0,2},{1,3},{2,0},{3,1},{4,6},{5,7},{6,4},{7,5},{8,10},{9,11},{10,... | collective-permute-start | bytes 1572872 | tf_op jit(solution)/shard_map/ppermute | solution.py:220
  41.6 0.4 collective-permute-done.5.refs_6_
  42.0 1.6 %collective-permute-start.17 = (bf16[2,4,64,512]{3,2,1,0:T(8,128)(2,1)}, bf16[2,4,64,512]{3,2,1,0:T(8,128)(2,1)S(1)}, u32[]{:S(2)}, u32[]{:S(2)}) collective-permute-start(bf16[2,4,64,512]{3,2,1,0:T(8,128)(2,1)} %get-tuple-element.12), channel_id=1, source_target_pairs={{0,3},{1,2},{2,1},{3,0},{4,7},{5,6},{6,5},{7,4},{8,11},{9,10},{10,... | collective-permute-start | bytes 1572872 | tf_op jit(solution)/shard_map/ppermute | solution.py:220
  43.6 0.1 collective-permute-start.6
  43.7 0.5 collective-permute-start.12
  44.2 1.0 %collective-permute-done.6.refs_7_ = bf16[128,1024]{1,0:T(8,128)(2,1)S(1)} collective-permute-done((bf16[128,1024]{1,0:T(8,128)(2,1)S(1)}, bf16[128,1024]{1,0:T(8,128)(2,1)S(1)}, u32[]{:S(2)}, u32[]{:S(2)}) %collective-permute-start.6) | collective-permute-done | bytes 262176 | tf_op jit(solution)/shard_map/ppermute | solution.py:220
  45.1 0.1 collective-permute-start.14
  46.0 6.7 %assemble.1.partial_ref = bf16[2,1024,512]{2,1,0:T(8,128)(2,1)} custom-call(s32[1]{0:T(128)S(6)} %copy.14.source_ref, s32[2,2]{1,0:T(2,128)} %op_ref.5, s32[16,128]{1,0:T(8,128)} %bitcast.5, bf16[128,1024]{1,0:T(8,128)(2,1)} %copy-done, bf16[128,1024]{1,0:T(8,128)(2,1)} %copy-done.4, bf16[128,1024]{1,0:T(8,128)(2,1)} %copy-done.3, ...), custom_call_target="tpu_custom_call" | custom-call | flops 1000 | bytes 1000 | tf_op jit(solution)/shard_map/assemble/pallas_call | solution.py:138
  52.7 2.3 %collective-permute-done.16.refs_6_ = bf16[2,4,64,512]{3,2,1,0:T(8,128)(2,1)S(1)} collective-permute-done((bf16[2,4,64,512]{3,2,1,0:T(8,128)(2,1)}, bf16[2,4,64,512]{3,2,1,0:T(8,128)(2,1)S(1)}, u32[]{:S(2)}, u32[]{:S(2)}) %collective-permute-start.16) | collective-permute-done | bytes 524320 | tf_op jit(solution)/shard_map/ppermute | solution.py:220
  55.0 10.1 %collective-permute-done.17.refs_7_ = bf16[2,4,64,512]{3,2,1,0:T(8,128)(2,1)S(1)} collective-permute-done((bf16[2,4,64,512]{3,2,1,0:T(8,128)(2,1)}, bf16[2,4,64,512]{3,2,1,0:T(8,128)(2,1)S(1)}, u32[]{:S(2)}, u32[]{:S(2)}) %collective-permute-start.17) | collective-permute-done | bytes 524320 | tf_op jit(solution)/shard_map/ppermute | solution.py:220
  65.1 0.8 %copy-done.14 = bf16[2,4,64,512]{3,2,1,0:T(8,128)(2,1)} copy-done((bf16[2,4,64,512]{3,2,1,0:T(8,128)(2,1)}, bf16[2,4,64,512]{3,2,1,0:T(8,128)(2,1)S(1)}, u32[]{:S(2)}) %copy-start.14) | copy-done | bytes 524312
  65.9 0.1 copy-done.18
  66.0 8.1 %contract.1 = bf16[2,4,32,2,2048]{4,3,2,1,0:T(2,128)(2,1)} custom-call(s32[1]{0:T(128)S(6)} %copy.14.source_ref, s32[2,2]{1,0:T(2,128)} %op_ref.5, s32[16,128]{1,0:T(8,128)} %bitcast.6, bf16[2,1024,512]{2,1,0:T(8,128)(2,1)} %assemble.1.partial_ref, bf16[128,1024]{1,0:T(8,128)(2,1)} %copy-done.15, bf16[128,1024]{1,0:T(8,128)(2,1)} %copy-done.17, ...), custom_call_target="tpu_custom_call" | custom-call | flops 2147483648 | tf_op jit(solution)/shard_map/contract/pallas_call | solution.py:194
  (48 shorter events, 0.2 us)
Async XLA Ops:
  1.5 38.2 %copy-start = (bf16[128,1024]{1,0:T(8,128)(2,1)}, bf16[128,1024]{1,0:T(8,128)(2,1)S(1)}, u32[]{:S(2)}) copy-start(bf16[128,1024]{1,0:T(8,128)(2,1)S(1)} %pad_maximum_fusion.refs_0_) | copy-start | bytes 786436
  1.5 12.4 %collective-permute-start.11 = (bf16[128,1024]{1,0:T(8,128)(2,1)S(1)}, bf16[128,1024]{1,0:T(8,128)(2,1)S(1)}, u32[]{:S(2)}, u32[]{:S(2)}) collective-permute-start(bf16[128,1024]{1,0:T(8,128)(2,1)S(1)} %pad_maximum_fusion.refs_0_), channel_id=1, source_target_pairs={{0,24},{4,28},{8,16},{12,20},{16,8},{20,12},{24,0},{28,4},{1,25},{... | collective-permute-start | bytes 786440 | tf_op jit(solution)/shard_map/ppermute | solution.py:220
  6.7 22.3 %collective-permute-start.7 = (bf16[128,1024]{1,0:T(8,128)(2,1)S(1)}, bf16[128,1024]{1,0:T(8,128)(2,1)S(1)}, u32[]{:S(2)}, u32[]{:S(2)}) collective-permute-start(bf16[128,1024]{1,0:T(8,128)(2,1)S(1)} %pad_maximum_fusion.refs_0_), channel_id=1, source_target_pairs={{0,16},{4,20},{8,24},{12,28},{16,0},{20,4},{24,8},{28,12},{1,17},{... | collective-permute-start | bytes 786440 | tf_op jit(solution)/shard_map/ppermute | solution.py:220
  6.7 23.8 %collective-permute-start.3 = (bf16[128,1024]{1,0:T(8,128)(2,1)S(1)}, bf16[128,1024]{1,0:T(8,128)(2,1)S(1)}, u32[]{:S(2)}, u32[]{:S(2)}) collective-permute-start(bf16[128,1024]{1,0:T(8,128)(2,1)S(1)} %pad_maximum_fusion.refs_0_), channel_id=1, source_target_pairs={{0,8},{4,12},{8,0},{12,4},{16,24},{20,28},{24,16},{28,20},{1,9},{5... | collective-permute-start | bytes 786440 | tf_op jit(solution)/shard_map/ppermute | solution.py:220
  7.3 23.2 %collective-permute-start.1 = (bf16[128,1024]{1,0:T(8,128)(2,1)S(1)}, bf16[128,1024]{1,0:T(8,128)(2,1)S(1)}, u32[]{:S(2)}, u32[]{:S(2)}) collective-permute-start(bf16[128,1024]{1,0:T(8,128)(2,1)S(1)} %pad_maximum_fusion.refs_0_), channel_id=1, source_target_pairs={{0,4},{4,0},{8,12},{12,8},{16,20},{20,16},{24,28},{28,24},{1,5},{5... | collective-permute-start | bytes 786440 | tf_op jit(solution)/shard_map/ppermute | solution.py:220
  8.9 22.2 %collective-permute-start = (bf16[128,1024]{1,0:T(8,128)(2,1)S(1)}, bf16[128,1024]{1,0:T(8,128)(2,1)S(1)}, u32[]{:S(2)}, u32[]{:S(2)}) collective-permute-start(bf16[128,1024]{1,0:T(8,128)(2,1)S(1)} %pad_maximum_fusion.refs_0_), channel_id=1, source_target_pairs={{0,1},{1,0},{2,3},{3,2},{4,5},{5,4},{6,7},{7,6},{8,9},{9,8},{10,11... | collective-permute-start | bytes 786440 | tf_op jit(solution)/shard_map/ppermute | solution.py:220
  13.9 29.7 %copy-start.15 = (bf16[128,1024]{1,0:T(8,128)(2,1)}, bf16[128,1024]{1,0:T(8,128)(2,1)S(1)}, u32[]{:S(2)}) copy-start(bf16[128,1024]{1,0:T(8,128)(2,1)S(1)} %collective-permute-done.11.refs_0_) | copy-start | bytes 786436
  13.9 17.3 %collective-permute-start.13 = (bf16[128,1024]{1,0:T(8,128)(2,1)S(1)}, bf16[128,1024]{1,0:T(8,128)(2,1)S(1)}, u32[]{:S(2)}, u32[]{:S(2)}) collective-permute-start(bf16[128,1024]{1,0:T(8,128)(2,1)S(1)} %collective-permute-done.11.refs_0_), channel_id=1, source_target_pairs={{0,4},{4,0},{8,12},{12,8},{16,20},{20,16},{24,28},{28,24},{1,5},{5... | collective-permute-start | bytes 786440 | tf_op jit(solution)/shard_map/ppermute | solution.py:220
  29.0 10.8 %copy-start.1 = (bf16[128,1024]{1,0:T(8,128)(2,1)}, bf16[128,1024]{1,0:T(8,128)(2,1)S(1)}, u32[]{:S(2)}) copy-start(bf16[128,1024]{1,0:T(8,128)(2,1)S(1)} %collective-permute-done.7.refs_8_) | copy-start | bytes 786436
  29.0 10.8 %collective-permute-start.9 = (bf16[128,1024]{1,0:T(8,128)(2,1)S(1)}, bf16[128,1024]{1,0:T(8,128)(2,1)S(1)}, u32[]{:S(2)}, u32[]{:S(2)}) collective-permute-start(bf16[128,1024]{1,0:T(8,128)(2,1)S(1)} %collective-permute-done.7.refs_8_), channel_id=1, source_target_pairs={{0,4},{4,0},{8,12},{12,8},{16,20},{20,16},{24,28},{28,24},{1,5},{5... | collective-permute-start | bytes 786440 | tf_op jit(solution)/shard_map/ppermute | solution.py:220
  30.5 9.3 %copy-start.2 = (bf16[128,1024]{1,0:T(8,128)(2,1)}, bf16[128,1024]{1,0:T(8,128)(2,1)S(1)}, u32[]{:S(2)}) copy-start(bf16[128,1024]{1,0:T(8,128)(2,1)S(1)} %collective-permute-done.3.refs_4_) | copy-start | bytes 786436
  30.5 9.6 %collective-permute-start.8 = (bf16[128,1024]{1,0:T(8,128)(2,1)S(1)}, bf16[128,1024]{1,0:T(8,128)(2,1)S(1)}, u32[]{:S(2)}, u32[]{:S(2)}) collective-permute-start(bf16[128,1024]{1,0:T(8,128)(2,1)S(1)} %collective-permute-done.7.refs_8_), channel_id=1, source_target_pairs={{0,1},{1,0},{2,3},{3,2},{4,5},{5,4},{6,7},{7,6},{8,9},{9,8},{10,11... | collective-permute-start | bytes 786440 | tf_op jit(solution)/shard_map/ppermute | solution.py:220
  30.5 9.3 %copy-start.3 = (bf16[128,1024]{1,0:T(8,128)(2,1)}, bf16[128,1024]{1,0:T(8,128)(2,1)S(1)}, u32[]{:S(2)}) copy-start(bf16[128,1024]{1,0:T(8,128)(2,1)S(1)} %collective-permute-done.1.refs_2_) | copy-start | bytes 786436
  30.5 11.5 %collective-permute-start.5 = (bf16[128,1024]{1,0:T(8,128)(2,1)S(1)}, bf16[128,1024]{1,0:T(8,128)(2,1)S(1)}, u32[]{:S(2)}, u32[]{:S(2)}) collective-permute-start(bf16[128,1024]{1,0:T(8,128)(2,1)S(1)} %collective-permute-done.3.refs_4_), channel_id=1, source_target_pairs={{0,4},{4,0},{8,12},{12,8},{16,20},{20,16},{24,28},{28,24},{1,5},{5... | collective-permute-start | bytes 786440 | tf_op jit(solution)/shard_map/ppermute | solution.py:220
  31.1 8.7 %copy-start.4 = (bf16[128,1024]{1,0:T(8,128)(2,1)}, bf16[128,1024]{1,0:T(8,128)(2,1)S(1)}, u32[]{:S(2)}) copy-start(bf16[128,1024]{1,0:T(8,128)(2,1)S(1)} %collective-permute-done.refs_1_) | copy-start | bytes 786436
  31.1 10.9 %collective-permute-start.4 = (bf16[128,1024]{1,0:T(8,128)(2,1)S(1)}, bf16[128,1024]{1,0:T(8,128)(2,1)S(1)}, u32[]{:S(2)}, u32[]{:S(2)}) collective-permute-start(bf16[128,1024]{1,0:T(8,128)(2,1)S(1)} %collective-permute-done.3.refs_4_), channel_id=1, source_target_pairs={{0,1},{1,0},{2,3},{3,2},{4,5},{5,4},{6,7},{7,6},{8,9},{9,8},{10,11... | collective-permute-start | bytes 786440 | tf_op jit(solution)/shard_map/ppermute | solution.py:220
  31.3 13.9 %copy-start.16 = (bf16[128,1024]{1,0:T(8,128)(2,1)}, bf16[128,1024]{1,0:T(8,128)(2,1)S(1)}, u32[]{:S(2)}) copy-start(bf16[128,1024]{1,0:T(8,128)(2,1)S(1)} %collective-permute-done.13.refs_2_) | copy-start | bytes 786436
  31.3 12.3 %collective-permute-start.2 = (bf16[128,1024]{1,0:T(8,128)(2,1)S(1)}, bf16[128,1024]{1,0:T(8,128)(2,1)S(1)}, u32[]{:S(2)}, u32[]{:S(2)}) collective-permute-start(bf16[128,1024]{1,0:T(8,128)(2,1)S(1)} %collective-permute-done.1.refs_2_), channel_id=1, source_target_pairs={{0,1},{1,0},{2,3},{3,2},{4,5},{5,4},{6,7},{7,6},{8,9},{9,8},{10,11... | collective-permute-start | bytes 786440 | tf_op jit(solution)/shard_map/ppermute | solution.py:220
  39.8 6.1 %copy-start.5 = (bf16[128,1024]{1,0:T(8,128)(2,1)}, bf16[128,1024]{1,0:T(8,128)(2,1)S(1)}, u32[]{:S(2)}) copy-start(bf16[128,1024]{1,0:T(8,128)(2,1)S(1)} %collective-permute-done.9.refs_10_) | copy-start | bytes 786436
  39.8 12.9 %collective-permute-start.15 = (bf16[2,4,64,512]{3,2,1,0:T(8,128)(2,1)}, bf16[2,4,64,512]{3,2,1,0:T(8,128)(2,1)S(1)}, u32[]{:S(2)}, u32[]{:S(2)}) collective-permute-start(bf16[2,4,64,512]{3,2,1,0:T(8,128)(2,1)} %get-tuple-element.10), channel_id=1, source_target_pairs={{0,1},{1,0},{2,3},{3,2},{4,5},{5,4},{6,7},{7,6},{8,9},{9,8},{10,11... | collective-permute-start | bytes 1572872 | tf_op jit(solution)/shard_map/ppermute | solution.py:220
  40.0 5.9 %copy-start.6 = (bf16[128,1024]{1,0:T(8,128)(2,1)}, bf16[128,1024]{1,0:T(8,128)(2,1)S(1)}, u32[]{:S(2)}) copy-start(bf16[128,1024]{1,0:T(8,128)(2,1)S(1)} %collective-permute-done.8.refs_9_) | copy-start | bytes 786436
  40.0 15.0 %collective-permute-start.16 = (bf16[2,4,64,512]{3,2,1,0:T(8,128)(2,1)}, bf16[2,4,64,512]{3,2,1,0:T(8,128)(2,1)S(1)}, u32[]{:S(2)}, u32[]{:S(2)}) collective-permute-start(bf16[2,4,64,512]{3,2,1,0:T(8,128)(2,1)} %get-tuple-element.11), channel_id=1, source_target_pairs={{0,2},{1,3},{2,0},{3,1},{4,6},{5,7},{6,4},{7,5},{8,10},{9,11},{10,... | collective-permute-start | bytes 1572872 | tf_op jit(solution)/shard_map/ppermute | solution.py:220
  41.9 4.0 %copy-start.7 = (bf16[128,1024]{1,0:T(8,128)(2,1)}, bf16[128,1024]{1,0:T(8,128)(2,1)S(1)}, u32[]{:S(2)}) copy-start(bf16[128,1024]{1,0:T(8,128)(2,1)S(1)} %collective-permute-done.5.refs_6_) | copy-start | bytes 786436
  41.9 1.7 %collective-permute-start.10 = (bf16[128,1024]{1,0:T(8,128)(2,1)S(1)}, bf16[128,1024]{1,0:T(8,128)(2,1)S(1)}, u32[]{:S(2)}, u32[]{:S(2)}) collective-permute-start(bf16[128,1024]{1,0:T(8,128)(2,1)S(1)} %collective-permute-done.9.refs_10_), channel_id=1, source_target_pairs={{0,1},{1,0},{2,3},{3,2},{4,5},{5,4},{6,7},{7,6},{8,9},{9,8},{10,11... | collective-permute-start | bytes 786440 | tf_op jit(solution)/shard_map/ppermute | solution.py:220
  42.0 4.0 %copy-start.8 = (bf16[128,1024]{1,0:T(8,128)(2,1)}, bf16[128,1024]{1,0:T(8,128)(2,1)S(1)}, u32[]{:S(2)}) copy-start(bf16[128,1024]{1,0:T(8,128)(2,1)S(1)} %collective-permute-done.4.refs_5_) | copy-start | bytes 786436
  42.0 23.1 %collective-permute-start.17 = (bf16[2,4,64,512]{3,2,1,0:T(8,128)(2,1)}, bf16[2,4,64,512]{3,2,1,0:T(8,128)(2,1)S(1)}, u32[]{:S(2)}, u32[]{:S(2)}) collective-permute-start(bf16[2,4,64,512]{3,2,1,0:T(8,128)(2,1)} %get-tuple-element.12), channel_id=1, source_target_pairs={{0,3},{1,2},{2,1},{3,0},{4,7},{5,6},{6,5},{7,4},{8,11},{9,10},{10,... | collective-permute-start | bytes 1572872 | tf_op jit(solution)/shard_map/ppermute | solution.py:220
  43.6 1.5 %collective-permute-start.6 = (bf16[128,1024]{1,0:T(8,128)(2,1)S(1)}, bf16[128,1024]{1,0:T(8,128)(2,1)S(1)}, u32[]{:S(2)}, u32[]{:S(2)}) collective-permute-start(bf16[128,1024]{1,0:T(8,128)(2,1)S(1)} %collective-permute-done.5.refs_6_), channel_id=1, source_target_pairs={{0,1},{1,0},{2,3},{3,2},{4,5},{5,4},{6,7},{7,6},{8,9},{9,8},{10,11... | collective-permute-start | bytes 786440 | tf_op jit(solution)/shard_map/ppermute | solution.py:220
  43.7 9.0 %collective-permute-start.12 = (bf16[128,1024]{1,0:T(8,128)(2,1)S(1)}, bf16[128,1024]{1,0:T(8,128)(2,1)S(1)}, u32[]{:S(2)}, u32[]{:S(2)}) collective-permute-start(bf16[128,1024]{1,0:T(8,128)(2,1)S(1)} %collective-permute-done.11.refs_0_), channel_id=1, source_target_pairs={{0,1},{1,0},{2,3},{3,2},{4,5},{5,4},{6,7},{7,6},{8,9},{9,8},{10,11... | collective-permute-start | bytes 786440 | tf_op jit(solution)/shard_map/ppermute | solution.py:220
  45.1 20.0 %collective-permute-start.14 = (bf16[128,1024]{1,0:T(8,128)(2,1)S(1)}, bf16[128,1024]{1,0:T(8,128)(2,1)S(1)}, u32[]{:S(2)}, u32[]{:S(2)}) collective-permute-start(bf16[128,1024]{1,0:T(8,128)(2,1)S(1)} %collective-permute-done.13.refs_2_), channel_id=1, source_target_pairs={{0,1},{1,0},{2,3},{3,2},{4,5},{5,4},{6,7},{7,6},{8,9},{9,8},{10,11... | collective-permute-start | bytes 786440 | tf_op jit(solution)/shard_map/ppermute | solution.py:220
  52.7 12.4 %copy-start.17 = (bf16[128,1024]{1,0:T(8,128)(2,1)}, bf16[128,1024]{1,0:T(8,128)(2,1)S(1)}, u32[]{:S(2)}) copy-start(bf16[128,1024]{1,0:T(8,128)(2,1)S(1)} %collective-permute-done.12.refs_1_) | copy-start | bytes 786436
  52.7 12.4 %copy-start.12 = (bf16[2,4,64,512]{3,2,1,0:T(8,128)(2,1)}, bf16[2,4,64,512]{3,2,1,0:T(8,128)(2,1)S(1)}, u32[]{:S(2)}) copy-start(bf16[2,4,64,512]{3,2,1,0:T(8,128)(2,1)S(1)} %collective-permute-done.15.refs_5_) | copy-start | bytes 1572868
  55.0 10.1 %copy-start.13 = (bf16[2,4,64,512]{3,2,1,0:T(8,128)(2,1)}, bf16[2,4,64,512]{3,2,1,0:T(8,128)(2,1)S(1)}, u32[]{:S(2)}) copy-start(bf16[2,4,64,512]{3,2,1,0:T(8,128)(2,1)S(1)} %collective-permute-done.16.refs_6_) | copy-start | bytes 1572868
  (5 other events, 7.2 us)
